TPU v7x, 512 devices: a whole 4x4x16 slice. The times are simulated.
512 devices in a mesh: dp: 8 (over z_hi, core), frame: 64 (over z_lo, y, x).
Axes of the slice: x: 4, y: 4, z: 16 (z_hi: 4, z_lo: 4; z = z_hi * 4 + z_lo), core: 2. Of those that a mesh axis runs over, the one named last changes fastest.
Arguments:
- queries: bfloat16 [262144, 576], P(('dp', 'frame')), may hold values from -6 to 6
- key_vectors: bfloat16 [262144, 576], P(('dp', 'frame')), may hold values from -6 to 6
- values: bfloat16 [262144, 576], P(('dp', 'frame')), may hold values from -6 to 6
- w_out: bfloat16 [576, 1152], P('frame'), may hold values from -0.25 to 0.25
- cotangent: bfloat16 [262144, 1152], P(('dp', 'frame')), may hold values from -24 to 24
Outputs:
- query_grad: bfloat16 [262144, 576], P(('dp', 'frame'))
- key_grad: bfloat16 [262144, 576], P(('dp', 'frame'))
- value_grad: bfloat16 [262144, 576], P(('dp', 'frame'))
- w_grad: bfloat16 [576, 1152], P('frame')
All inputs are finite; a program needn't handle non-finite values.
Results may differ from a plain program's by a relative error of at most 0.012.
Values may be sent and summed in bfloat16 or wider, within the bound.
A program may use at most 64 MiB of HBM per device.

v0:
```python
import math

import jax
import jax.numpy as jnp
from jax import lax
from jax.sharding import PartitionSpec as P

HS = 72
HEADS = 8
PT = 256


def attend_forward(queries, key_vectors, values, softmax_scale):
    scores = (
        jnp.einsum("blhs,bmhs->bhlm", queries, key_vectors, preferred_element_type=jnp.float32)
        * softmax_scale
    )
    probabilities = jax.nn.softmax(scores, axis=-1)
    mixture = jnp.einsum(
        "bhlm,bmhs->blhs",
        probabilities.astype(jnp.bfloat16),
        values,
        preferred_element_type=jnp.float32,
    )
    return mixture.astype(jnp.bfloat16)


def attend_backward(queries, key_vectors, values, upstream, softmax_scale):
    scores = (
        jnp.einsum("blhs,bmhs->bhlm", queries, key_vectors, preferred_element_type=jnp.float32)
        * softmax_scale
    )
    probabilities = jax.nn.softmax(scores, axis=-1)
    weights_low = probabilities.astype(jnp.bfloat16)
    grad_probs = jnp.einsum("blhs,bmhs->bhlm", upstream, values, preferred_element_type=jnp.float32)
    value_grad = jnp.einsum(
        "bhlm,blhs->bmhs", weights_low, upstream, preferred_element_type=jnp.float32
    ).astype(jnp.bfloat16)
    row_inner = jnp.sum(probabilities * grad_probs, axis=-1, keepdims=True)
    grad_scores = (probabilities * (grad_probs - row_inner)).astype(jnp.bfloat16)
    query_grad = (
        jnp.einsum("bhlm,bmhs->blhs", grad_scores, key_vectors, preferred_element_type=jnp.float32)
        * softmax_scale
    ).astype(jnp.bfloat16)
    key_grad = (
        jnp.einsum("bhlm,blhs->bmhs", grad_scores, queries, preferred_element_type=jnp.float32)
        * softmax_scale
    ).astype(jnp.bfloat16)
    return (query_grad, key_grad, value_grad)


def on_device(queries, key_vectors, values, w_out, cotangent):
    token_rows = queries.shape[0]
    half_heads = HEADS // 2
    side_width = half_heads * HS
    frame_devices = lax.axis_size("frame")
    clip_count = token_rows // PT
    per_device = PT // frame_devices
    softmax_scale = 1.0 / math.sqrt(HS)

    def spatial_view(array):
        return array[:, :side_width].reshape(clip_count, PT, half_heads, HS)

    def temporal_view(array):
        return array[:, side_width:].reshape(clip_count, frame_devices, per_device, 1, side_width)

    def sequences(array):
        return array.reshape(array.shape[0] * array.shape[2], array.shape[3], half_heads, HS)

    def positions_back(array, like):
        return array.reshape(like.shape[0], 1, like.shape[2], like.shape[3], side_width)

    upstream = lax.dot_general(
        cotangent,
        lax.all_gather(w_out, "frame", axis=0, tiled=True),
        (((1,), (1,)), ((), ())),
        preferred_element_type=jnp.float32,
    ).astype(jnp.bfloat16)
    upstream_view = temporal_view(upstream)
    query_here = lax.all_to_all(
        temporal_view(queries), "frame", split_axis=1, concat_axis=3, tiled=True
    )
    key_here = lax.all_to_all(
        temporal_view(key_vectors), "frame", split_axis=1, concat_axis=3, tiled=True
    )
    value_here = lax.all_to_all(
        temporal_view(values), "frame", split_axis=1, concat_axis=3, tiled=True
    )
    mixture = attend_forward(
        sequences(query_here), sequences(key_here), sequences(value_here), softmax_scale
    )
    back_rows = lax.all_to_all(
        positions_back(mixture, query_here), "frame", split_axis=3, concat_axis=1, tiled=True
    )
    upstream_pos = lax.all_to_all(upstream_view, "frame", split_axis=1, concat_axis=3, tiled=True)
    grads_here = attend_backward(
        sequences(query_here),
        sequences(key_here),
        sequences(value_here),
        sequences(upstream_pos),
        softmax_scale,
    )
    grads_pos = tuple((positions_back(single, upstream_pos) for single in grads_here))
    temporal_grads = (
        lax.all_to_all(grads_pos[0], "frame", split_axis=3, concat_axis=1, tiled=True),
        lax.all_to_all(grads_pos[1], "frame", split_axis=3, concat_axis=1, tiled=True),
        lax.all_to_all(grads_pos[2], "frame", split_axis=3, concat_axis=1, tiled=True),
    )
    spatial_out = attend_forward(
        spatial_view(queries), spatial_view(key_vectors), spatial_view(values), softmax_scale
    )
    attended = jnp.concatenate(
        [spatial_out.reshape(token_rows, side_width), back_rows.reshape(token_rows, side_width)],
        axis=1,
    )
    inv_root = 1.0 / math.sqrt(token_rows * lax.axis_size("dp") * frame_devices)
    share_rows = w_out.shape[0]
    local_grad = lax.dot_general(
        attended, cotangent, (((0,), (0,)), ((), ())), preferred_element_type=jnp.float32
    )
    total_grad = lax.psum(local_grad, ("dp", "frame"))
    summed = lax.dynamic_slice_in_dim(
        total_grad, lax.axis_index("frame") * share_rows, share_rows, 0
    )
    w_grad = (summed * inv_root).astype(jnp.bfloat16)
    spatial_grads = attend_backward(
        spatial_view(queries),
        spatial_view(key_vectors),
        spatial_view(values),
        spatial_view(upstream),
        softmax_scale,
    )

    def joined(index_of):
        return jnp.concatenate(
            [
                spatial_grads[index_of].reshape(token_rows, side_width),
                temporal_grads[index_of].reshape(token_rows, side_width),
            ],
            axis=1,
        )

    return (joined(0), joined(1), joined(2), w_grad)


def solution(mesh):
    placed = (
        P(("dp", "frame"), None),
        P(("dp", "frame"), None),
        P(("dp", "frame"), None),
        P("frame", None),
        P(("dp", "frame"), None),
    )
    return jax.shard_map(
        on_device,
        mesh=mesh,
        in_specs=placed,
        out_specs=(
            P(("dp", "frame"), None),
            P(("dp", "frame"), None),
            P(("dp", "frame"), None),
            P("frame", None),
        ),
        check_vma=False,
    )
```

profile of v0, /device:TPU:1, one launch (start us, length us, event | category | flops | bytes accessed | tf_op | source)
XLA Modules:
  0.0 963.6 jit_solution(12936788392046772155)
XLA Ops:
  8.0 1.9 fusion.69
  11.2 12.6 %all-to-all-start = ((bf16[2,64,4,1,288]{4,2,0,3,1:T(4,128)(2,1)}), bf16[2,64,4,1,288]{4,2,0,3,1:T(4,128)(2,1)S(1)}, u32[]{:S(2)}, u32[]{:S(2)}) async-start(bf16[2,64,4,1,288]{4,2,0,3,1:T(4,128)(2,1)} %copy.71), calls=%async_computation | async-start | bytes 786432 | tf_op jit(solution)/shard_map/all_to_all | solution.py:80
  26.5 10.4 %all-to-all-done = bf16[2,64,4,1,288]{4,2,0,3,1:T(4,128)(2,1)S(1)} async-done(((bf16[2,64,4,1,288]{4,2,0,3,1:T(4,128)(2,1)}), bf16[2,64,4,1,288]{4,2,0,3,1:T(4,128)(2,1)S(1)}, u32[]{:S(2)}, u32[]{:S(2)}) %all-to-all-start) | async-done | bytes 294944 | tf_op jit(solution)/shard_map/all_to_all | solution.py:80
  36.9 6.5 all-to-all-start.1
  46.4 9.5 all-to-all-done.1
  56.0 7.4 all-to-all-start.3
  63.3 277.6 %all-gather.3.cloned.1.call-done = bf16[64,9,1152]{2,1,0:T(8,128)(2,1)} async-done(((bf16[1,9,1152]{2,1,0:T(8,128)(2,1)}), bf16[64,9,1152]{2,1,0:T(8,128)(2,1)}) %all-gather.3.cloned.1.call-update) | async-done | bytes 1327120 | tf_op jit(solution)/shard_map/all_gather | solution.py:75
  341.0 3.7 reshape.125
  344.7 2.3 convolution_convert_fusion
  348.9 9.0 all-to-all-start.2
  364.9 4.8 all-to-all-done.2
  369.6 5.6 all-to-all-start.7
  379.9 3.7 fusion.78
  388.1 10.0 %all-to-all-start.6 = ((bf16[2,1,4,64,288]{4,2,0,1,3:T(4,128)(2,1)}), bf16[2,1,4,64,288]{4,2,0,1,3:T(4,128)(2,1)S(1)}, u32[]{:S(2)}, u32[]{:S(2)}) async-start(bf16[2,1,4,64,288]{4,2,0,1,3:T(4,128)(2,1)} %reshape.128), calls=%async_computation.6 | async-start | bytes 786432 | tf_op jit(solution)/shard_map/all_to_all | solution.py:107
  398.1 1.9 fusion.14
  402.3 2.2 multiply_reduce_fusion.2
  406.8 3.0 all-to-all-done.6
  409.8 7.2 all-to-all-start.5
  417.1 3.4 fusion.18
  422.3 3.8 multiply_reduce_fusion
  429.7 10.4 %all-to-all-start.4 = ((bf16[2,1,4,64,288]{4,2,0,1,3:T(4,128)(2,1)}), bf16[2,1,4,64,288]{4,2,0,1,3:T(4,128)(2,1)S(1)}, u32[]{:S(2)}, u32[]{:S(2)}) async-start(bf16[2,1,4,64,288]{4,2,0,1,3:T(4,128)(2,1)} %reshape.126), calls=%async_computation.4 | async-start | bytes 786432 | tf_op jit(solution)/shard_map/all_to_all | solution.py:105
  440.1 2.6 multiply_convert_fusion
  444.5 504.9 %all-reduce.2.cloned.1.call-done = f32[576,1152]{1,0:T(8,128)} async-done(((f32[576,1152]{1,0:T(8,128)}), f32[576,1152]{1,0:T(8,128)}) %all-reduce.2.cloned.1.call-update) | async-done | bytes 2654224 | tf_op jit(solution)/shard_map/psum | solution.py:121
  953.2 1.9 pad_maximum_fusion.2
  (96 shorter events, 41.3 us)
Async XLA Ops:
  8.0 336.7 %copy-start = (bf16[512,1152]{1,0:T(8,128)(2,1)S(1)}, bf16[512,1152]{1,0:T(8,128)(2,1)}, u32[]{:S(2)}) copy-start(bf16[512,1152]{1,0:T(8,128)(2,1)} %param.9) | copy-start | bytes 3538948
  8.0 16.4 %copy-start.7 = (bf16[512,576]{0,1:T(8,128)(2,1)S(1)}, bf16[512,576]{0,1:T(8,128)(2,1)}, u32[]{:S(2)}) copy-start(bf16[512,576]{0,1:T(8,128)(2,1)} %param.6) | copy-start | bytes 1769476
  11.2 25.7 %all-to-all-start = ((bf16[2,64,4,1,288]{4,2,0,3,1:T(4,128)(2,1)}), bf16[2,64,4,1,288]{4,2,0,3,1:T(4,128)(2,1)S(1)}, u32[]{:S(2)}, u32[]{:S(2)}) async-start(bf16[2,64,4,1,288]{4,2,0,3,1:T(4,128)(2,1)} %copy.71), calls=%async_computation | async-start | bytes 786432 | tf_op jit(solution)/shard_map/all_to_all | solution.py:80
  23.7 317.2 %all-gather.3.cloned.1.call-start = ((), (), s32[]{:S(2)}) async-start(), calls=%async_computation.9 | async-start | bytes 2396160 | tf_op jit(solution)/shard_map/all_gather | solution.py:75
  36.9 19.1 %all-to-all-start.1 = ((bf16[2,64,4,1,288]{4,2,0,3,1:T(4,128)(2,1)}), bf16[2,64,4,1,288]{4,2,0,3,1:T(4,128)(2,1)S(1)}, u32[]{:S(2)}, u32[]{:S(2)}) async-start(bf16[2,64,4,1,288]{4,2,0,3,1:T(4,128)(2,1)} %copy.74), calls=%async_computation.1 | async-start | bytes 786432 | tf_op jit(solution)/shard_map/all_to_all | solution.py:83
  56.0 293.0 %all-to-all-start.3 = ((bf16[2,64,4,1,288]{4,2,0,3,1:T(4,128)(2,1)}), bf16[2,64,4,1,288]{4,2,0,3,1:T(4,128)(2,1)S(1)}, u32[]{:S(2)}, u32[]{:S(2)}) async-start(bf16[2,64,4,1,288]{4,2,0,3,1:T(4,128)(2,1)} %copy.82), calls=%async_computation.3 | async-start | bytes 786432 | tf_op jit(solution)/shard_map/all_to_all | solution.py:86
  348.9 20.7 %all-to-all-start.2 = ((bf16[2,64,4,1,288]{4,2,0,3,1:T(4,128)(2,1)}), bf16[2,64,4,1,288]{4,2,0,3,1:T(4,128)(2,1)S(1)}, u32[]{:S(2)}, u32[]{:S(2)}) async-start(bf16[2,64,4,1,288]{4,2,0,3,1:T(4,128)(2,1)} %copy.79), calls=%async_computation.2 | async-start | bytes 786432 | tf_op jit(solution)/shard_map/all_to_all | solution.py:95
  359.9 1.6 copy-start.8
  369.6 18.5 %all-to-all-start.7 = ((bf16[2,1,4,64,288]{4,2,0,1,3:T(4,128)(2,1)}), bf16[2,1,4,64,288]{4,2,0,1,3:T(4,128)(2,1)S(1)}, u32[]{:S(2)}, u32[]{:S(2)}) async-start(bf16[2,1,4,64,288]{4,2,0,1,3:T(4,128)(2,1)} %reshape.129), calls=%async_computation.7 | async-start | bytes 786432 | tf_op jit(solution)/shard_map/all_to_all | solution.py:92
  376.3 7.4 copy-start.2
  384.0 0.8 copy-start.9
  388.1 21.7 %all-to-all-start.6 = ((bf16[2,1,4,64,288]{4,2,0,1,3:T(4,128)(2,1)}), bf16[2,1,4,64,288]{4,2,0,1,3:T(4,128)(2,1)S(1)}, u32[]{:S(2)}, u32[]{:S(2)}) async-start(bf16[2,1,4,64,288]{4,2,0,1,3:T(4,128)(2,1)} %reshape.128), calls=%async_computation.6 | async-start | bytes 786432 | tf_op jit(solution)/shard_map/all_to_all | solution.py:107
  402.3 2.2 copy-start.6
  404.8 12.3 %copy-start.10 = (bf16[36,8,2,256]{3,1,2,0:T(8,128)(2,1)S(1)}, bf16[36,8,2,256]{3,1,2,0:T(8,128)(2,1)}, u32[]{:S(2)}) copy-start(bf16[36,8,2,256]{3,1,2,0:T(8,128)(2,1)} %copy.142) | copy-start | bytes 884740
  409.8 19.9 %all-to-all-start.5 = ((bf16[2,1,4,64,288]{4,2,0,1,3:T(4,128)(2,1)}), bf16[2,1,4,64,288]{4,2,0,1,3:T(4,128)(2,1)S(1)}, u32[]{:S(2)}, u32[]{:S(2)}) async-start(bf16[2,1,4,64,288]{4,2,0,1,3:T(4,128)(2,1)} %reshape.127), calls=%async_computation.5 | async-start | bytes 786432 | tf_op jit(solution)/shard_map/all_to_all | solution.py:106
  417.0 532.4 %all-reduce.2.cloned.1.call-start = ((), (), s32[]{:S(2)}) async-start(), calls=%async_computation.8 | async-start | bytes 5308416 | tf_op jit(solution)/shard_map/psum | solution.py:121
  420.5 1.0 copy-start.5
  420.5 1.7 copy-start.12
  422.3 3.8 copy-start.1
  422.3 3.8 copy-start.11
  429.7 523.0 %all-to-all-start.4 = ((bf16[2,1,4,64,288]{4,2,0,1,3:T(4,128)(2,1)}), bf16[2,1,4,64,288]{4,2,0,1,3:T(4,128)(2,1)S(1)}, u32[]{:S(2)}, u32[]{:S(2)}) async-start(bf16[2,1,4,64,288]{4,2,0,1,3:T(4,128)(2,1)} %reshape.126), calls=%async_computation.4 | async-start | bytes 786432 | tf_op jit(solution)/shard_map/all_to_all | solution.py:105
  440.1 2.6 copy-start.4
  442.7 1.0 copy-start.3
Sparse Core Ops, SparseCore 0:
  26.6 314.2 all-gather.2
Sparse Core Ops, SparseCore 1:
  422.9 526.5 all-reduce.1
where the time goes:
time: 966 us; the launch traced here: 964 us
  waiting for transfers between devices  811 us (84%)
  starting transfers between devices  68.8 us (7%)
  local copies, waits for them, and re-layouts  36.5 us (4%)
  matrix products  24.1 us (2%)
  between operations  15.9 us (2%)
    psum x1, waiting for transfers between devices, on_device(): total_grad = lax.psum(local_grad, ('dp', 'frame'))  505 us
    all_gather x1, waiting for transfers between devices, on_device(): lax.all_gather(w_out, 'frame', axis=0, tiled=True)  278 us
  transfers between devices with their start and end apart: 10, of which 6 were waited for; matrix products, arithmetic and copies ran while one was open for 6% of the time, Pallas kernels for 0%

commit v1 on v0

v1 whole, which is shorter than its diff:
```python
import math

import jax
import jax.numpy as jnp
import numpy as np
from jax import lax
from jax.experimental import pallas as pl
from jax.experimental.pallas import tpu as pltpu
from jax.sharding import PartitionSpec as P

HS = 72
HEADS = 8
PT = 256
D = 1152
HW = 576
ROWS = 512
SIDE = 288
PAIR = 144
MSG = 640
CUT = 384
BACK = 256
WIN = 640
OFF = 512
SHARE = 9
F = 64
MESH = pl.DeviceIdType.MESH
BF = jnp.bfloat16
F32 = jnp.float32

(W_Z, W_Y, W_X, W_C, SEND_A, SEND_B, BACK_A, BACK_B, G_C0, G_X0, G_Y0, G_C1, G_X1, G_Y1, G_Z, G_H, G_F, OWN) = range(18)
STAGES = 18


def group_rows():
    m = np.zeros((256, 256), np.float32)
    for g in range(4):
        for f in range(16):
            for s in range(4):
                m[64 * g + 4 * f + s, 16 * f + 4 * g + s] = 1
    return m


def w_after_z():
    m = np.zeros((48, 64), np.float32)
    for z in range(4):
        for i in range(SHARE):
            m[z * SHARE + i, z * 16 + i] = 1
    return m


def w_after_y():
    m = np.zeros((144, 192), np.float32)
    for y in range(4):
        for r in range(36):
            m[y * 36 + r, y * 48 + r] = 1
    return m


def upstream_columns():
    m = np.zeros((HW, HW), np.float32)
    for x in range(4):
        for y in range(4):
            for z in range(4):
                for i in range(SHARE):
                    m[x * 144 + y * 36 + z * 9 + i, (z * 16 + y * 4 + x) * 9 + i] = 1
    return m


def attended_columns():
    m = np.zeros((SIDE, 320), np.float32)
    for x in range(4):
        for y in range(4):
            for zz in range(2):
                for i in range(SHARE):
                    m[(zz * 16 + y * 4 + x) * 9 + i, x * 80 + y * 18 + zz * 9 + i] = 1
    return m


def grad_after_x():
    m = np.zeros((128, 80), np.float32)
    for y in range(4):
        for r in range(18):
            m[y * 32 + r, y * 18 + r] = 1
    return m


def grad_after_y():
    m = np.zeros((64, 64), np.float32)
    for h in range(2):
        for zz in range(2):
            for i in range(SHARE):
                m[(2 * h + zz) * 16 + i, h * 32 + zz * 9 + i] = 1
    return m


def dot(a, b, ca, cb):
    return lax.dot_general(a, b, (((ca,), (cb,)), ((), ())), preferred_element_type=F32)


def move(m, a):
    return dot(m, a, 1, 0).astype(BF)


def probs_of(q, k, scale, keep):
    s = dot(k, q, 1, 1) * scale
    if keep is not None:
        s = jnp.where(keep, s, -1e30)
    e = jnp.exp(s - jnp.max(s, axis=0, keepdims=True))
    return e / jnp.sum(e, axis=0, keepdims=True)


def attend(p, q, k, v, u, scale):
    p16 = p.astype(BF)
    att = dot(p16, v, 0, 0).astype(BF)
    dv = dot(p16, u, 1, 0).astype(BF)
    dp = dot(v, u, 1, 1)
    ds = (p * (dp - jnp.sum(p * dp, axis=0, keepdims=True))).astype(BF)
    dk = (dot(ds, q, 1, 0) * scale).astype(BF)
    dq = (dot(ds, k, 0, 0) * scale).astype(BF)
    return att, dv, dq, dk


def kernel(
    q_ref, k_ref, v_ref, w_ref, cot_ref,
    rows_m, wz_m, wy_m, up_m, att_m, gx_m, gy_m,
    dq_ref, dk_ref, dv_ref, wg_ref,
    wpad, g1, c1, g2, c2, wall, up, msg, got, grp, prob, res, out_msg, back,
    att, part, rc, xs, rx, ys, ry, zs, zp, rz, rh, fw,
    send, recv,
):
    me, d = lax.axis_index("frame"), lax.axis_index("dp")
    core, zhi = lax.rem(d, 2), lax.div(d, 2)
    x, y, z = lax.rem(me, 4), lax.rem(lax.div(me, 4), 4), lax.div(me, 16)
    scale = 1.0 / math.sqrt(HS)
    win = pl.multiple_of(core * OFF, 128)
    other_win = pl.multiple_of((1 - core) * OFF, 128)
    give = pl.multiple_of(core * WIN, 128)

    def rows16(i, n=16):
        return pl.ds(pl.multiple_of(i * n, 16), n)

    def frame(p):
        return {"frame": p}

    def on_x(i):
        return frame(me - x + lax.rem(x + i, 4))

    def on_y(i):
        return frame(me + 4 * (lax.rem(y + i, 4) - y))

    def on_z(i):
        return frame(me + 16 * (lax.rem(z + i, 4) - z))

    def on_zhi(i):
        return {"dp": lax.rem(d + 2 * i, 8)}

    sibling = {"dp": d + 1 - 2 * core}

    def put(src, dst, stage, to):
        pltpu.make_async_remote_copy(
            src_ref=src, dst_ref=dst, send_sem=send.at[stage], recv_sem=recv.at[stage],
            device_id=to, device_id_type=MESH,
        ).start()

    def arrived(ref, stage):
        pltpu.make_async_copy(ref, ref, recv.at[stage]).wait()

    def sent(ref, stage):
        pltpu.make_async_copy(ref, ref, send.at[stage]).wait()

    barrier = pltpu.get_barrier_semaphore()

    def greet(i, c):
        pl.semaphore_signal(barrier, inc=1, device_id=frame(lax.rem(me + i, F)), device_id_type=MESH)
        return c

    lax.fori_loop(1, F, greet, 0)
    for i in range(1, 4):
        pl.semaphore_signal(barrier, inc=1, device_id=on_zhi(i), device_id_type=MESH)
    pl.semaphore_signal(barrier, inc=1, device_id=sibling, device_id_type=MESH)

    wpad[...] = jnp.zeros_like(wpad)
    wpad[0:SHARE, :] = w_ref[:, pl.ds(win, WIN)]
    msg[:, :, HW:MSG] = jnp.zeros((2, ROWS, MSG - HW), BF)
    for hp in range(2):
        cols = slice(SIDE + PAIR * hp, SIDE + PAIR * (hp + 1))
        msg[hp, :, 0:PAIR] = q_ref[:, cols]
        msg[hp, :, PAIR : 2 * PAIR] = k_ref[:, cols]
        msg[hp, :, 2 * PAIR : 3 * PAIR] = v_ref[:, cols]

    pl.semaphore_wait(barrier, F - 1 + 4)

    for i in range(1, 4):
        put(wpad, g1.at[rows16(z)], W_Z, on_z(i))
    g1[rows16(z), :] = wpad[...]

    def send_messages(lo, hi, stage, first, last):
        def body(i, c):
            p = lax.rem(me + i, F)
            put(
                msg.at[lax.rem(p, 2), rows16(lax.div(p, 2)), lo:hi],
                got.at[rows16(me), lo:hi],
                stage,
                frame(p),
            )
            return c

        lax.fori_loop(first, last, body, 0)

    send_messages(0, CUT, SEND_A, 1, 22)
    arrived(g1.at[0:48], W_Z)
    c1[...] = move(wz_m[...], g1[...])
    for i in range(1, 4):
        put(c1, g2.at[rows16(y, 48)], W_Y, on_y(i))
    g2[rows16(y, 48), :] = c1[...]
    send_messages(0, CUT, SEND_A, 22, 43)
    arrived(g2.at[0:144], W_Y)
    c2[...] = move(wy_m[...], g2[...])
    for i in range(1, 4):
        put(c2, wall.at[rows16(x, 144), pl.ds(win, WIN)], W_X, on_x(i))
    wall[rows16(x, 144), pl.ds(win, WIN)] = c2[...]
    send_messages(0, CUT, SEND_A, 43, F)
    arrived(wall.at[0:432, 0:WIN], W_X)
    put(wall.at[:, pl.ds(give, OFF)], wall.at[:, pl.ds(give, OFF)], W_C, sibling)
    arrived(wall.at[:, 0:OFF], W_C)

    for r in range(2):
        here = slice(256 * r, 256 * (r + 1))
        u = dot(cot_ref[here, :], wall[...], 1, 1).astype(BF)
        u = dot(u, up_m[...], 1, 0).astype(BF)
        up[here, :] = u
        for hp in range(2):
            msg[hp, here, 3 * PAIR : HW] = u[:, SIDE + PAIR * hp : SIDE + PAIR * (hp + 1)]
    send_messages(CUT, MSG, SEND_B, 1, F)

    def clip(c, carry):
        here = pl.ds(pl.multiple_of(c * PT, PT), PT)
        for h in range(HEADS // 2):
            cols = slice(h * HS, (h + 1) * HS)
            q, k, v, u = q_ref[here, cols], k_ref[here, cols], v_ref[here, cols], up[here, cols]
            p = probs_of(q, k, scale, None)
            att[here, cols], dv_ref[here, cols], dq_ref[here, cols], dk_ref[here, cols] = attend(
                p, q, k, v, u, scale
            )
        return carry

    lax.fori_loop(0, 2, clip, 0)

    def grad_core(h, stage):
        moved = dot(att[...], att_m[...], 1, 0).astype(BF)
        part[h] = dot(moved, cot_ref[...], 0, 0).astype(BF)
        put(part.at[h, :, pl.ds(other_win, WIN)], rc.at[h], stage, sibling)

    def grad_x(h, stage):
        arrived(rc.at[h], stage)
        xs[h] = (part[h, :, pl.ds(win, WIN)].astype(F32) + rc[h].astype(F32)).astype(BF)
        for i in range(1, 4):
            to = lax.rem(x + i, 4)
            put(xs.at[h, rows16(to, 80)], rx.at[h, x], stage + 1, on_x(i))
        rx[h, x] = xs[h, rows16(x, 80), :]

    def total(ref, h):
        t = ref[h, 0].astype(F32)
        for i in range(1, 4):
            t = t + ref[h, i].astype(F32)
        return t

    def grad_y(h, stage):
        arrived(rx.at[h, 0:3], stage + 1)
        ys[h] = move(gx_m[...], total(rx, h).astype(BF))
        for i in range(1, 4):
            to = lax.rem(y + i, 4)
            put(ys.at[h, rows16(to, 32)], ry.at[h, y], stage + 2, on_y(i))
        ry[h, y] = ys[h, rows16(y, 32), :]

    def grad_sum(h, stage):
        arrived(ry.at[h, 0:3], stage + 2)
        zs[32 * h : 32 * (h + 1), :] = total(ry, h).astype(BF)

    grad_core(0, G_C0)

    mine = pltpu.make_async_copy(
        msg.at[lax.rem(me, 2), rows16(lax.div(me, 2))], got.at[rows16(me)], recv.at[OWN]
    )
    mine.start()
    mine.wait()
    arrived(got.at[0 : 16 * (F - 1), 0:CUT], SEND_A)

    def regroup(lo, hi):
        def body(c, carry):
            t = move(rows_m[...], got[rows16(c, 256), lo:hi])
            for g in range(4):
                grp[g, rows16(c, 64), lo:hi] = t[64 * g : 64 * (g + 1), :]
            return carry

        lax.fori_loop(0, 4, body, 0)

    keep = lax.rem(lax.broadcasted_iota(jnp.int32, (256, 256), 0), 4) == lax.rem(
        lax.broadcasted_iota(jnp.int32, (256, 256), 1), 4
    )

    regroup(0, CUT)

    def group_probs(g, carry):
        for b in range(2):
            q = grp[g, :, b * HS : (b + 1) * HS]
            k = grp[g, :, PAIR + b * HS : PAIR + (b + 1) * HS]
            prob[g, b] = probs_of(q, k, scale, keep)
        return carry

    lax.fori_loop(0, 4, group_probs, 0)

    grad_x(0, G_C0)

    arrived(got.at[0 : 16 * (F - 1), CUT:MSG], SEND_B)
    regroup(CUT, MSG)

    def group_grads(g, carry):
        for b in range(2):
            def cols(n):
                return slice(n * PAIR + b * HS, n * PAIR + (b + 1) * HS)

            q, k, v, u = (grp[g, :, cols(n)] for n in range(4))
            got_all = attend(prob[g, b], q, k, v, u, scale)
            for n in range(4):
                res[g, :, cols(n)] = got_all[n]
        return carry

    res[:, :, HW:MSG] = jnp.zeros((4, 256, MSG - HW), BF)
    lax.fori_loop(0, 4, group_grads, 0)

    def ungroup(c, carry):
        t = jnp.concatenate([res[g, rows16(c, 64), :] for g in range(4)], axis=0)
        out_msg[rows16(c, 256), :] = dot(rows_m[...], t, 0, 0).astype(BF)
        return carry

    lax.fori_loop(0, 4, ungroup, 0)

    def send_back(lo, hi, stage):
        def body(i, c):
            p = lax.rem(me + i, F)
            put(
                out_msg.at[rows16(p), lo:hi],
                back.at[lax.rem(me, 2), rows16(lax.div(me, 2)), lo:hi],
                stage,
                frame(p),
            )
            return c

        lax.fori_loop(1, F, body, 0)

    send_back(0, BACK, BACK_A)
    send_back(BACK, MSG, BACK_B)
    mine = pltpu.make_async_copy(
        out_msg.at[rows16(me)], back.at[lax.rem(me, 2), rows16(lax.div(me, 2))], recv.at[OWN]
    )
    mine.start()
    mine.wait()

    grad_y(0, G_C0)

    arrived(got.at[0 : 16 * (F - 1), 0:BACK], BACK_A)
    for hp in range(2):
        att[:, hp * PAIR : (hp + 1) * PAIR] = back[hp, :, 0:PAIR]
    grad_core(1, G_C1)
    grad_sum(0, G_C0)
    grad_x(1, G_C1)
    grad_y(1, G_C1)
    grad_sum(1, G_C1)

    zp[...] = move(gy_m[...], zs[...])
    for i in range(1, 4):
        put(zp.at[rows16(lax.rem(z + i, 4))], rz.at[0, z], G_Z, on_z(i))
    rz[0, z] = zp[rows16(z), :]
    arrived(rz.at[0, 0:3], G_Z)
    rh[0, zhi] = total(rz, 0)
    for i in range(1, 4):
        put(rh.at[0, zhi], rh.at[0, zhi], G_H, on_zhi(i))
    arrived(rh.at[0, 0:3], G_H)
    fw[:, pl.ds(win, WIN)] = total(rh, 0)
    put(fw.at[:, pl.ds(give, OFF)], fw.at[:, pl.ds(give, OFF)], G_F, sibling)

    arrived(got.at[0 : 16 * (F - 1), BACK:MSG], BACK_B)
    for hp in range(2):
        cols = slice(SIDE + PAIR * hp, SIDE + PAIR * (hp + 1))
        dv_ref[:, cols] = back[hp, :, PAIR : 2 * PAIR]
        dq_ref[:, cols] = back[hp, :, 2 * PAIR : 3 * PAIR]
        dk_ref[:, cols] = back[hp, :, 3 * PAIR : HW]

    arrived(fw.at[:, 0:OFF], G_F)
    wg_ref[...] = (fw[0:SHARE, :] * (1.0 / math.sqrt(ROWS * F * 8))).astype(BF)

    sent(g1.at[0:48], W_Z)
    sent(g2.at[0:144], W_Y)
    sent(wall.at[0:432, 0:WIN], W_X)
    sent(wall.at[:, 0:OFF], W_C)
    sent(got.at[0 : 16 * (F - 1), 0:CUT], SEND_A)
    sent(got.at[0 : 16 * (F - 1), CUT:MSG], SEND_B)
    sent(got.at[0 : 16 * (F - 1), 0:BACK], BACK_A)
    sent(got.at[0 : 16 * (F - 1), BACK:MSG], BACK_B)
    for h, stage in ((0, G_C0), (1, G_C1)):
        sent(rc.at[h], stage)
        sent(rx.at[h, 0:3], stage + 1)
        sent(ry.at[h, 0:3], stage + 2)
    sent(rz.at[0, 0:3], G_Z)
    sent(rh.at[0, 0:3], G_H)
    sent(fw.at[:, 0:OFF], G_F)


def on_device(queries, key_vectors, values, w_out, cotangent):
    tables = [
        jnp.asarray(m(), BF)
        for m in (group_rows, w_after_z, w_after_y, upstream_columns, attended_columns, grad_after_x, grad_after_y)
    ]
    vmem = pl.BlockSpec(memory_space=pltpu.VMEM)
    side = jax.ShapeDtypeStruct((ROWS, HW), BF)
    scratch = [
        ((16, WIN), BF),
        ((64, WIN), BF),
        ((48, WIN), BF),
        ((192, WIN), BF),
        ((144, WIN), BF),
        ((HW, D), BF),
        ((ROWS, HW), BF),
        ((2, ROWS, MSG), BF),
        ((16 * F, MSG), BF),
        ((4, 256, MSG), BF),
        ((4, 2, 256, 256), F32),
        ((4, 256, MSG), BF),
        ((16 * F, MSG), BF),
        ((2, ROWS, MSG), BF),
        ((ROWS, SIDE), BF),
        ((2, 320, D), BF),
        ((2, 320, WIN), BF),
        ((2, 320, WIN), BF),
        ((2, 4, 80, WIN), BF),
        ((2, 128, WIN), BF),
        ((2, 4, 32, WIN), BF),
        ((64, WIN), BF),
        ((64, WIN), BF),
        ((1, 4, 16, WIN), BF),
        ((1, 4, 16, WIN), F32),
        ((16, D), F32),
    ]
    return pl.pallas_call(
        kernel,
        out_shape=(side, side, side, jax.ShapeDtypeStruct((SHARE, D), BF)),
        in_specs=[vmem] * 12,
        out_specs=(vmem,) * 4,
        scratch_shapes=[pltpu.VMEM(s, t) for s, t in scratch]
        + [pltpu.SemaphoreType.DMA((STAGES,)), pltpu.SemaphoreType.DMA((STAGES,))],
        compiler_params=pltpu.CompilerParams(
            collective_id=0, has_side_effects=True, vmem_limit_bytes=56 * 1024 * 1024
        ),
        cost_estimate=pl.CostEstimate(flops=4_000_000_000, bytes_accessed=6_000_000, transcendentals=2_000_000),
    )(queries, key_vectors, values, w_out, cotangent, *tables)


def solution(mesh):
    rows = P(("dp", "frame"), None)
    return jax.shard_map(
        on_device,
        mesh=mesh,
        in_specs=(rows, rows, rows, P("frame", None), rows),
        out_specs=(rows, rows, rows, P("frame", None)),
        check_vma=False,
    )
```

time: 966 us -> 133 us (0.14)
  waiting for transfers between devices: 811 us -> 0 us
  Pallas kernels: 0 us -> 123 us
  starting transfers between devices: 68.8 us -> 0 us
  local copies, waits for them, and re-layouts: 36.5 us -> 9.4 us
  matrix products: 24.1 us -> 0 us
  between operations: 15.9 us -> 0.68 us
    psum x1 -> x0, waiting for transfers between devices: 505 us -> none  [on_device(): total_grad = lax.psum(local_grad, ('dp', 'frame'))]
    all_gather x1 -> x0, waiting for transfers between devices: 278 us -> none  [on_device(): lax.all_gather(w_out, 'frame', axis=0, tiled=True)]
    pallas_call x0 -> x1, Pallas kernels: none -> 123 us  [on_device(): pl.pallas_call(kernel, out_shape=(side, side, side, jax.ShapeDtypeStruct(...]
    all_to_all x8 -> x0, starting transfers between devices: 68.7 us -> none  [the longest x1 12.6 us: on_device(): lax.all_to_all(temporal_view(queries), 'frame', split_axis=1, concat_axis...]
    all_to_all x8 -> x0, waiting for transfers between devices: 27.7 us -> none  [the longest x1 10.4 us: on_device(): lax.all_to_all(temporal_view(queries), 'frame', split_axis=1, concat_axis...]
    reshape x32 -> x0, local copies, waits for them, and re-layouts: 21.3 us -> none  [the longest x8 6.69 us: positions_back(): array.reshape(like.shape[0], 1, like.shape[2], like.shape[3], side_width)]
    dot_general x12 -> x0, matrix products: 18.7 us -> none  [the longest x2 6.01 us: attend_backward(): jnp.einsum('blhs,bmhs->bhlm', upstream, values, preferred_element_type=jn...]
  transfers between devices with their start and end apart: 10 -> 0, of which waited for: 6 -> 0; matrix products, arithmetic and copies ran while one was open for 6% -> 0% of each run, Pallas kernels for 0% -> 0%
where the time goes in v1:
time: 133 us
  Pallas kernels  123 us (92%)
  local copies, waits for them, and re-layouts  9.4 us (7%)
    pallas_call x1, Pallas kernels, on_device(): pl.pallas_call(kernel, out_shape=(side, side, side, jax.ShapeDtypeStruct(...  123 us
    unnamed x14, local copies, waits for them, and re-layouts  5.06 us
    pallas_call x3, local copies, waits for them, and re-layouts, on_device(): pl.pallas_call(kernel, out_shape=(side, side, side, jax.ShapeDtypeStruct(...  4.34 us

profile of v1, /device:TPU:1, one launch (start us, length us, event | category | flops | bytes accessed | tf_op | source)
XLA Modules:
  0.0 133.0 jit_solution(7310065190759363393)
XLA Ops:
  0.6 0.0 copy-start.3
  0.6 0.0 copy-start.2
  0.7 2.2 %copy.16.q_ref = bf16[512,576]{1,0:T(8,128)(2,1)} copy(bf16[512,576]{0,1:T(8,128)(2,1)} %param.12) | data formatting | bytes 1179648 | tf_op args[0]
  2.9 0.0 copy-done.2
  2.9 1.1 copy.17.k_ref
  4.0 0.0 copy-done.3
  4.0 1.1 copy.18.v_ref
  5.1 122.9 %shard_map.147 = (bf16[512,576]{1,0:T(8,128)(2,1)}, bf16[512,576]{1,0:T(8,128)(2,1)}, bf16[512,576]{1,0:T(8,128)(2,1)}, bf16[9,1152]{1,0:T(8,128)(2,1)}) custom-call(bf16[512,576]{1,0:T(8,128)(2,1)} %copy.16.q_ref, bf16[512,576]{1,0:T(8,128)(2,1)} %copy.17.k_ref, bf16[512,576]{1,0:T(8,128)(2,1)} %copy.18.v_ref, bf16[9,1152]{1,0:T(8,128)(2,1)} %w_ref.1, ...), custom_call_target="tpu_custom_call" | custom-call | flops 4000000000 | bytes 6000000 | tf_op jit(solution)/shard_map/pallas_call | solution.py:445
  128.0 0.0 copy-start.1
  128.0 0.0 copy-start
  128.0 2.2 %copy.19 = bf16[512,576]{0,1:T(8,128)(2,1)} copy(bf16[512,576]{1,0:T(8,128)(2,1)} %get-tuple-element.4) | data formatting | bytes 1179648 | tf_op jit(solution)/shard_map/pallas_call | solution.py:445
  130.3 0.0 copy-done.1
  130.3 0.0 copy-start.4
  130.3 1.1 copy.20
  131.3 0.0 copy-done
  131.3 1.1 copy.21
  132.4 0.0 copy-done.4
  132.4 0.6 copy.23
Async XLA Ops:
  0.6 3.3 %copy-start.3 = (bf16[512,576]{0,1:T(8,128)(2,1)S(1)}, bf16[512,576]{0,1:T(8,128)(2,1)}, u32[]{:S(2)}) copy-start(bf16[512,576]{0,1:T(8,128)(2,1)} %param.14) | copy-start | bytes 1769476
  0.6 2.3 %copy-start.2 = (bf16[512,576]{0,1:T(8,128)(2,1)S(1)}, bf16[512,576]{0,1:T(8,128)(2,1)}, u32[]{:S(2)}) copy-start(bf16[512,576]{0,1:T(8,128)(2,1)} %param.13) | copy-start | bytes 1769476
  128.0 2.3 %copy-start.1 = (bf16[512,576]{1,0:T(8,128)(2,1)S(1)}, bf16[512,576]{1,0:T(8,128)(2,1)}, u32[]{:S(2)}) copy-start(bf16[512,576]{1,0:T(8,128)(2,1)} %get-tuple-element.5) | copy-start | bytes 1769476
  128.0 3.3 %copy-start = (bf16[512,576]{1,0:T(8,128)(2,1)S(1)}, bf16[512,576]{1,0:T(8,128)(2,1)}, u32[]{:S(2)}) copy-start(bf16[512,576]{1,0:T(8,128)(2,1)} %get-tuple-element.6) | copy-start | bytes 1769476
  130.3 2.1 %copy-start.4 = (bf16[9,1152]{1,0:T(8,128)(2,1)S(1)}, bf16[9,1152]{1,0:T(8,128)(2,1)}, u32[]{:S(2)}) copy-start(bf16[9,1152]{1,0:T(8,128)(2,1)} %get-tuple-element.15) | copy-start | bytes 62212

commit v2 on v1

v2 whole, which is shorter than its diff:
```python
import math

import jax
import jax.numpy as jnp
import numpy as np
from jax import lax
from jax.experimental import pallas as pl
from jax.experimental.pallas import tpu as pltpu
from jax.sharding import PartitionSpec as P

HS = 72
HEADS = 8
PT = 256
D = 1152
HW = 576
ROWS = 512
SIDE = 288
PAIR = 144
MSG = 640
CUT1, CUT2 = 384, 512
BACK = 256
WIN = 640
OFF = 512
SHARE = 9
F = 64
MESH = pl.DeviceIdType.MESH
BF = jnp.bfloat16
F32 = jnp.float32

(
    W_Z, W_Y0, W_X0, W_C0, W_Y1, W_X1, W_C1, SEND_A, SEND_B, SEND_C, BACK_A, BACK_B,
    G_C0, G_X0, G_Y0, G_C1, G_X1, G_Y1, G_Z, G_H, G_F, OWN, LOAD,
) = range(23)
STAGES = 40

ATT, DV, DQ, DK = (0, 72), (144, 360), (216, 432), (288, 504)


def group_rows():
    m = np.zeros((256, 256), np.float32)
    for g in range(4):
        for f in range(16):
            for s in range(4):
                m[64 * g + 4 * f + s, 16 * f + 4 * g + s] = 1
    return m


def side_rows():
    m = np.zeros((320, SIDE), np.float32)
    for x in range(4):
        for y in range(4):
            for zz in range(2):
                for i in range(SHARE):
                    m[x * 80 + y * 18 + zz * 9 + i, (zz * 16 + y * 4 + x) * 9 + i] = 1
    return m


def spread_y():
    m = np.zeros((128, 80), np.float32)
    for y in range(4):
        for r in range(18):
            m[y * 32 + r, y * 18 + r] = 1
    return m


def spread_z():
    m = np.zeros((64, 64), np.float32)
    for h in range(2):
        for zz in range(2):
            for i in range(SHARE):
                m[(2 * h + zz) * 16 + i, h * 32 + zz * 9 + i] = 1
    return m


def dot(a, b, ca, cb):
    return lax.dot_general(a, b, (((ca,), (cb,)), ((), ())), preferred_element_type=F32)


def move(m, a):
    return dot(m, a, 1, 0).astype(BF)


def softmax_down(s, keep):
    if keep is not None:
        s = jnp.where(keep, s, -1e30)
    e = jnp.exp(s - jnp.max(s, axis=0, keepdims=True))
    return e / jnp.sum(e, axis=0, keepdims=True)


def score_grads(p, dp):
    return (p * (dp - jnp.sum(p * dp, axis=0, keepdims=True))).astype(BF)


def kernel(
    q_hbm, k_hbm, v_hbm, w_ref, cot_hbm,
    rows_m, side_m, side_t, gx_m, gx_t, gy_m, gy_t,
    dq_hbm, dk_hbm, dv_hbm, wg_ref,
    q_ref, k_ref, v_ref, cot_ref, dq_ref, dk_ref, dv_ref,
    wpad, g1, c1, g2, c2, wall, up, msg_t, msg, got, grp, prob, sprob, res, out_msg, back,
    att, part, rc, xs, rx, ys, ry, zs, zp, rz, rh, fw,
    send, recv,
):
    me, d = lax.axis_index("frame"), lax.axis_index("dp")
    core, zhi = lax.rem(d, 2), lax.div(d, 2)
    x, y, z = lax.rem(me, 4), lax.rem(lax.div(me, 4), 4), lax.div(me, 16)
    me_hp, me_row = lax.rem(me, 2), lax.div(me, 2)
    scale = 1.0 / math.sqrt(HS)
    win = pl.multiple_of(core * OFF, 128)
    other_win = pl.multiple_of((1 - core) * OFF, 128)
    give = pl.multiple_of(core * WIN, 128)

    def rows16(i, n=16):
        return pl.ds(pl.multiple_of(i * n, 16), n)

    def frame(p):
        return {"frame": p}

    def on_x(i):
        return frame(me - x + lax.rem(x + i, 4))

    def on_y(i):
        return frame(me + 4 * (lax.rem(y + i, 4) - y))

    def on_z(i):
        return frame(me + 16 * (lax.rem(z + i, 4) - z))

    def on_zhi(i):
        return {"dp": lax.rem(d + 2 * i, 8)}

    sibling = {"dp": d + 1 - 2 * core}

    def put(src, dst, stage, to):
        pltpu.make_async_remote_copy(
            src_ref=src, dst_ref=dst, send_sem=send.at[stage], recv_sem=recv.at[stage],
            device_id=to, device_id_type=MESH,
        ).start()

    def arrived(ref, stage):
        pltpu.make_async_copy(ref, ref, recv.at[stage]).wait()

    def sent(ref, stage):
        pltpu.make_async_copy(ref, ref, send.at[stage]).wait()

    barrier = pltpu.get_barrier_semaphore()

    def greet(i, c):
        pl.semaphore_signal(barrier, inc=1, device_id=frame(lax.rem(me + i, F)), device_id_type=MESH)
        return c

    lax.fori_loop(1, F, greet, 0)
    for i in range(1, 4):
        pl.semaphore_signal(barrier, inc=1, device_id=on_zhi(i), device_id_type=MESH)
    pl.semaphore_signal(barrier, inc=1, device_id=sibling, device_id_type=MESH)

    tops, bottoms = slice(0, SIDE), slice(SIDE, HW)
    loads = []
    for n, (src, dst, part_rows) in enumerate(
        [(a, b, bottoms) for a, b in ((q_hbm, q_ref), (k_hbm, k_ref), (v_hbm, v_ref))]
        + [(a, b, tops) for a, b in ((q_hbm, q_ref), (k_hbm, k_ref), (v_hbm, v_ref))]
        + [(cot_hbm, cot_ref, slice(0, ROWS))]
    ):
        loads.append(pltpu.make_async_copy(src.at[part_rows], dst.at[part_rows], recv.at[LOAD + n]))
        loads[-1].start()

    wpad[...] = jnp.zeros_like(wpad)
    wpad[0:SHARE, :] = w_ref[:, pl.ds(win, WIN)]
    msg_t[:, HW:MSG, :] = jnp.zeros((2, MSG - HW, ROWS), BF)
    for n in range(3):
        loads[n].wait()
    for hp in range(2):
        rows = slice(SIDE + PAIR * hp, SIDE + PAIR * (hp + 1))
        for n, ref in enumerate((q_ref, k_ref, v_ref)):
            msg_t[hp, n * PAIR : (n + 1) * PAIR, :] = ref[rows, :]
        msg[hp, :, 0:CUT1] = msg_t[hp, 0:CUT1, :].T

    pl.semaphore_wait(barrier, F - 1 + 4)

    for i in range(1, 4):
        put(wpad, g1.at[rows16(z)], W_Z, on_z(i))
    g1[rows16(z), :] = wpad[...]

    def send_messages(lo, hi, stage, first, last):
        def to(row, hp):
            put(msg.at[hp, rows16(row), lo:hi], got.at[rows16(me), lo:hi], stage, frame(2 * row + hp))

        def body(i, c):
            row = lax.rem(me_row + i, F // 2)
            to(row, 0)
            to(row, 1)
            return c

        if first == 0:
            to(me_row, 1 - me_hp)
            first = 1
        lax.fori_loop(first, last, body, 0)

    def w_y(h):
        for i in range(1, 4):
            put(c1.at[32 * h : 32 * (h + 1)], g2.at[h, rows16(y, 32)], W_Y0 + 3 * h, on_y(i))
        g2[h, rows16(y, 32), :] = c1[32 * h : 32 * (h + 1), :]

    def w_x(h):
        arrived(g2.at[h, 0:96], W_Y0 + 3 * h)
        c2[h] = move(gx_t[...], g2[h])
        for i in range(1, 4):
            put(c2.at[h], wall.at[h, rows16(x, 80), pl.ds(win, WIN)], W_X0 + 3 * h, on_x(i))
        wall[h, rows16(x, 80), pl.ds(win, WIN)] = c2[h]

    def w_core(h):
        arrived(wall.at[h, 0:240, 0:WIN], W_X0 + 3 * h)
        both = wall.at[h, :, pl.ds(give, OFF)]
        put(both, both, W_C0 + 3 * h, sibling)

    def upstream(h):
        arrived(wall.at[h, :, 0:OFF], W_C0 + 3 * h)
        u = dot(wall[h], cot_ref[...], 1, 1).astype(BF)
        return move(side_t[...], u)

    send_messages(0, CUT1, SEND_A, 0, 11)
    arrived(g1.at[0:48], W_Z)
    c1[...] = move(gy_t[...], g1[...])
    w_y(1)
    w_y(0)
    send_messages(0, CUT1, SEND_A, 11, 21)
    w_x(1)
    w_x(0)
    send_messages(0, CUT1, SEND_A, 21, F // 2)
    for n in range(3, 7):
        loads[n].wait()

    def clip_columns(c):
        return pl.ds(pl.multiple_of(c * PT, PT), PT)

    def head_rows(h):
        return slice(h * HS, (h + 1) * HS)

    def clip_forward(c, carry):
        here = clip_columns(c)
        for h in range(HEADS // 2):
            rows = head_rows(h)
            p = softmax_down(dot(k_ref[rows, here], q_ref[rows, here], 0, 0) * scale, None)
            sprob[c, h] = p
            att[rows, here] = dot(v_ref[rows, here], p.astype(BF), 1, 0).astype(BF)
        return carry

    def clip_backward(c, carry):
        here = clip_columns(c)
        for h in range(HEADS // 2):
            rows = head_rows(h)
            q, k, v, u = q_ref[rows, here], k_ref[rows, here], v_ref[rows, here], up[rows, here]
            p = sprob[c, h]
            dv_ref[rows, here] = dot(u, p.astype(BF), 1, 1).astype(BF)
            ds = score_grads(p, dot(v, u, 0, 0))
            dq_ref[rows, here] = (dot(k, ds, 1, 0) * scale).astype(BF)
            dk_ref[rows, here] = (dot(q, ds, 1, 1) * scale).astype(BF)
        return carry

    def grad_core(h, moved, stage):
        part[h] = dot(moved.astype(BF), cot_ref[...], 1, 0).astype(BF)
        put(part.at[h, :, pl.ds(other_win, WIN)], rc.at[h], stage, sibling)

    def grad_x(h, stage):
        arrived(rc.at[h], stage)
        xs[h] = (part[h, :, pl.ds(win, WIN)].astype(F32) + rc[h].astype(F32)).astype(BF)
        for i in range(1, 4):
            put(xs.at[h, rows16(lax.rem(x + i, 4), 80)], rx.at[h, x], stage + 1, on_x(i))
        rx[h, x] = xs[h, rows16(x, 80), :]

    def total(ref, h):
        t = ref[h, 0].astype(F32)
        for i in range(1, 4):
            t = t + ref[h, i].astype(F32)
        return t

    def grad_y(h, stage):
        arrived(rx.at[h, 0:3], stage + 1)
        ys[h] = move(gx_m[...], total(rx, h).astype(BF))
        for i in range(1, 4):
            put(ys.at[h, rows16(lax.rem(y + i, 4), 32)], ry.at[h, y], stage + 2, on_y(i))
        ry[h, y] = ys[h, rows16(y, 32), :]

    def grad_sum(h, stage):
        arrived(ry.at[h, 0:3], stage + 2)
        zs[32 * h : 32 * (h + 1), :] = total(ry, h).astype(BF)

    lax.fori_loop(0, 2, clip_forward, 0)
    w_core(1)
    grad_core(0, dot(side_m[...], att[...], 1, 0), G_C0)

    msg_t_up = upstream(1)
    for hp in range(2):
        msg_t[hp, 3 * PAIR : HW, :] = msg_t_up[hp * PAIR : (hp + 1) * PAIR, :]
        msg[hp, :, CUT1:MSG] = msg_t[hp, CUT1:MSG, :].T
    send_messages(CUT1, CUT2, SEND_B, 0, F // 2)
    w_core(0)
    send_messages(CUT2, MSG, SEND_C, 0, F // 2)

    mine = pltpu.make_async_copy(msg.at[me_hp, rows16(me_row)], got.at[rows16(me)], recv.at[OWN])
    mine.start()
    mine.wait()

    def regroup(lo, hi):
        def body(c, carry):
            t = move(rows_m[...], got[rows16(c, 256), lo:hi])
            for g in range(4):
                grp[g, rows16(c, 64), lo:hi] = t[64 * g : 64 * (g + 1), :]
            return carry

        lax.fori_loop(0, 4, body, 0)

    def ungroup(lo, hi):
        def body(c, carry):
            t = jnp.concatenate([res[g, rows16(c, 64), lo:hi] for g in range(4)], axis=0)
            out_msg[rows16(c, 256), lo:hi] = dot(rows_m[...], t, 0, 0).astype(BF)
            return carry

        lax.fori_loop(0, 4, body, 0)

    def send_back(lo, hi, stage, first, last):
        def to(row, hp):
            p = 2 * row + hp
            put(out_msg.at[rows16(p), lo:hi], back.at[me_hp, rows16(me_row), lo:hi], stage, frame(p))

        def body(i, c):
            row = lax.rem(me_row + i, F // 2)
            to(row, 0)
            to(row, 1)
            return c

        if first == 0:
            to(me_row, 1 - me_hp)
            first = 1
        lax.fori_loop(first, last, body, 0)

    keep = lax.rem(lax.broadcasted_iota(jnp.int32, (256, 256), 0), 4) == lax.rem(
        lax.broadcasted_iota(jnp.int32, (256, 256), 1), 4
    )

    def part_of(g, n, b):
        return grp[g, :, n * PAIR + b * HS : n * PAIR + (b + 1) * HS]

    def group_probs(g, carry):
        for b in range(2):
            prob[g, b] = softmax_down(dot(part_of(g, 1, b), part_of(g, 0, b), 1, 1) * scale, keep)
        return carry

    def group_attended(g, carry):
        for b in range(2):
            res[g, :, ATT[b] : ATT[b] + HS] = dot(prob[g, b].astype(BF), part_of(g, 2, b), 0, 0).astype(BF)
        return carry

    def group_grads(b):
        def body(g, carry):
            q, k, v, u = (part_of(g, n, b) for n in range(4))
            p = prob[g, b]
            res[g, :, DV[b] : DV[b] + HS] = dot(p.astype(BF), u, 1, 0).astype(BF)
            ds = score_grads(p, dot(v, u, 1, 1))
            res[g, :, DQ[b] : DQ[b] + HS] = (dot(ds, k, 0, 0) * scale).astype(BF)
            res[g, :, DK[b] : DK[b] + HS] = (dot(ds, q, 1, 0) * scale).astype(BF)
            return carry

        lax.fori_loop(0, 4, body, 0)

    res[:, :, HW:MSG] = jnp.zeros((4, 256, MSG - HW), BF)
    arrived(got.at[0 : 16 * (F - 1), 0:CUT1], SEND_A)
    regroup(0, CUT1)
    lax.fori_loop(0, 4, group_probs, 0)
    grad_x(0, G_C0)

    arrived(got.at[0 : 16 * (F - 1), CUT1:CUT2], SEND_B)
    regroup(CUT1, CUT2)
    lax.fori_loop(0, 4, group_attended, 0)
    group_grads(0)
    ungroup(0, BACK)
    send_back(0, BACK, BACK_A, 0, F // 2)

    arrived(got.at[0 : 16 * (F - 1), CUT2:MSG], SEND_C)
    regroup(CUT2, MSG)
    group_grads(1)
    ungroup(BACK, MSG)
    mine = pltpu.make_async_copy(out_msg.at[rows16(me)], back.at[me_hp, rows16(me_row)], recv.at[OWN])
    mine.start()
    mine.wait()

    grad_y(0, G_C0)
    up[...] = upstream(0)
    clip_backward(0, 0)

    sent(got.at[0 : 16 * (F - 1), 0:BACK], BACK_A)
    send_back(BACK, MSG, BACK_B, 0, 11)
    arrived(got.at[0 : 16 * (F - 1), 0:BACK], BACK_A)
    grad_core(
        1,
        dot(side_m[:, 0:PAIR], back[0, :, 0:PAIR], 1, 1) + dot(side_m[:, PAIR:SIDE], back[1, :, 0:PAIR], 1, 1),
        G_C1,
    )
    send_back(BACK, MSG, BACK_B, 11, 21)
    grad_sum(0, G_C0)
    grad_x(1, G_C1)
    send_back(BACK, MSG, BACK_B, 21, F // 2)
    clip_backward(1, 0)
    grad_y(1, G_C1)
    stores = []
    for n, (src, dst) in enumerate(((dq_ref, dq_hbm), (dk_ref, dk_hbm), (dv_ref, dv_hbm))):
        stores.append(pltpu.make_async_copy(src.at[tops], dst.at[tops], recv.at[LOAD + 7 + n]))
        stores[-1].start()
    grad_sum(1, G_C1)

    zp[...] = move(gy_m[...], zs[...])
    for i in range(1, 4):
        put(zp.at[rows16(lax.rem(z + i, 4))], rz.at[0, z], G_Z, on_z(i))
    rz[0, z] = zp[rows16(z), :]
    arrived(rz.at[0, 0:3], G_Z)
    rh[0, zhi] = total(rz, 0).astype(BF)
    for i in range(1, 4):
        put(rh.at[0, zhi], rh.at[0, zhi], G_H, on_zhi(i))

    arrived(got.at[0 : 16 * (F - 1), BACK:MSG], BACK_B)
    for hp in range(2):
        t = back[hp, :, 128:MSG].T
        for b in range(2):
            first = SIDE + PAIR * hp + HS * b
            for ref, at in ((dv_ref, DV), (dq_ref, DQ), (dk_ref, DK)):
                ref[first : first + HS, :] = t[at[b] - 128 : at[b] - 128 + HS, :]
    for n, (src, dst) in enumerate(((dq_ref, dq_hbm), (dk_ref, dk_hbm), (dv_ref, dv_hbm))):
        stores.append(pltpu.make_async_copy(src.at[bottoms], dst.at[bottoms], recv.at[LOAD + 10 + n]))
        stores[-1].start()

    arrived(rh.at[0, 0:3], G_H)
    fw[:, pl.ds(win, WIN)] = total(rh, 0)
    both = fw.at[:, pl.ds(give, OFF)]
    put(both, both, G_F, sibling)
    arrived(fw.at[:, 0:OFF], G_F)
    wg_ref[...] = (fw[0:SHARE, :] * (1.0 / math.sqrt(ROWS * F * 8))).astype(BF)

    sent(g1.at[0:48], W_Z)
    for h in range(2):
        sent(g2.at[h, 0:96], W_Y0 + 3 * h)
        sent(wall.at[h, 0:240, 0:WIN], W_X0 + 3 * h)
        sent(wall.at[h, :, 0:OFF], W_C0 + 3 * h)
    sent(got.at[0 : 16 * (F - 1), 0:CUT1], SEND_A)
    sent(got.at[0 : 16 * (F - 1), CUT1:CUT2], SEND_B)
    sent(got.at[0 : 16 * (F - 1), CUT2:MSG], SEND_C)
    sent(got.at[0 : 16 * (F - 1), BACK:MSG], BACK_B)
    for h, stage in ((0, G_C0), (1, G_C1)):
        sent(rc.at[h], stage)
        sent(rx.at[h, 0:3], stage + 1)
        sent(ry.at[h, 0:3], stage + 2)
    sent(rz.at[0, 0:3], G_Z)
    sent(rh.at[0, 0:3], G_H)
    sent(fw.at[:, 0:OFF], G_F)
    for copy in stores:
        copy.wait()


def on_device(queries, key_vectors, values, w_out, cotangent):
    tables = [
        jnp.asarray(m, BF)
        for m in (
            group_rows(), side_rows(), side_rows().T, spread_y(), spread_y().T, spread_z(), spread_z().T,
        )
    ]
    vmem, hbm = pl.BlockSpec(memory_space=pltpu.VMEM), pl.BlockSpec(memory_space=pl.ANY)
    turned = jax.ShapeDtypeStruct((HW, ROWS), BF)
    scratch = (
        [((HW, ROWS), BF)] * 3
        + [((ROWS, D), BF)]
        + [((HW, ROWS), BF)] * 3
        + [
            ((16, WIN), BF),
            ((64, WIN), BF),
            ((64, WIN), BF),
            ((2, 128, WIN), BF),
            ((2, 80, WIN), BF),
            ((2, 320, D), BF),
            ((SIDE, ROWS), BF),
            ((2, MSG, ROWS), BF),
            ((2, ROWS, MSG), BF),
            ((16 * F, MSG), BF),
            ((4, 256, MSG), BF),
            ((4, 2, 256, 256), F32),
            ((2, 4, 256, 256), F32),
            ((4, 256, MSG), BF),
            ((16 * F, MSG), BF),
            ((2, ROWS, MSG), BF),
            ((SIDE, ROWS), BF),
            ((2, 320, D), BF),
            ((2, 320, WIN), BF),
            ((2, 320, WIN), BF),
            ((2, 4, 80, WIN), BF),
            ((2, 128, WIN), BF),
            ((2, 4, 32, WIN), BF),
            ((64, WIN), BF),
            ((64, WIN), BF),
            ((1, 4, 16, WIN), BF),
            ((1, 4, 16, WIN), BF),
            ((16, D), F32),
        ]
    )
    dq, dk, dv, wg = pl.pallas_call(
        kernel,
        out_shape=(turned, turned, turned, jax.ShapeDtypeStruct((SHARE, D), BF)),
        in_specs=[hbm] * 3 + [vmem, hbm] + [vmem] * 7,
        out_specs=(hbm, hbm, hbm, vmem),
        scratch_shapes=[pltpu.VMEM(s, t) for s, t in scratch]
        + [pltpu.SemaphoreType.DMA((STAGES,)), pltpu.SemaphoreType.DMA((STAGES,))],
        compiler_params=pltpu.CompilerParams(
            collective_id=0, has_side_effects=True, vmem_limit_bytes=56 * 1024 * 1024
        ),
        cost_estimate=pl.CostEstimate(flops=4_000_000_000, bytes_accessed=6_000_000, transcendentals=2_000_000),
    )(queries.T, key_vectors.T, values.T, w_out, cotangent, *tables)
    return dq.T, dk.T, dv.T, wg


def solution(mesh):
    rows = P(("dp", "frame"), None)
    return jax.shard_map(
        on_device,
        mesh=mesh,
        in_specs=(rows, rows, rows, P("frame", None), rows),
        out_specs=(rows, rows, rows, P("frame", None)),
        check_vma=False,
    )
```

time: 133 us -> 111 us (0.83)
  Pallas kernels: 123 us -> 106 us
  local copies, waits for them, and re-layouts: 9.4 us -> 4.27 us
    pallas_call x1, Pallas kernels: 123 us -> 106 us  [on_device(): pl.pallas_call(kernel, out_shape=(turned, turned, turned, jax.ShapeDtypeS...]
    pallas_call x3 -> x0, local copies, waits for them, and re-layouts: 4.34 us -> none  [on_device(): pl.pallas_call(kernel, out_shape=(side, side, side, jax.ShapeDtypeStruct(...]
    unnamed x14 -> x10, local copies, waits for them, and re-layouts: 5.06 us -> 4.27 us
where the time goes in v2:
time: 111 us
  Pallas kernels  106 us (95%)
  local copies, waits for them, and re-layouts  4.27 us (4%)
    pallas_call x1, Pallas kernels, on_device(): pl.pallas_call(kernel, out_shape=(turned, turned, turned, jax.ShapeDtypeS...  106 us
    unnamed x10, local copies, waits for them, and re-layouts  4.27 us

profile of v2, /device:TPU:1, one launch (start us, length us, event | category | flops | bytes accessed | tf_op | source)
XLA Modules:
  0.0 110.9 jit_solution(4926973818271373589)
XLA Ops:
  0.6 106.0 %shard_map.147 = (bf16[576,512]{1,0:T(8,128)(2,1)}, bf16[576,512]{1,0:T(8,128)(2,1)}, bf16[576,512]{1,0:T(8,128)(2,1)}, bf16[9,1152]{1,0:T(8,128)(2,1)}) custom-call(bf16[576,512]{1,0:T(8,128)(2,1)} %bitcast.9, bf16[576,512]{1,0:T(8,128)(2,1)} %bitcast.10, bf16[576,512]{1,0:T(8,128)(2,1)} %bitcast.11, bf16[9,1152]{1,0:T(8,128)(2,1)} %w_ref.1, ...), custom_call_target="tpu_custom_call" | custom-call | flops 4000000000 | bytes 6000000 | tf_op jit(solution)/shard_map/pallas_call | solution.py:500
  106.6 0.0 copy-start.1
  106.6 0.0 copy-start
  106.7 2.0 %copy.20 = bf16[512,576]{0,1:T(8,128)(2,1)} copy(bf16[512,576]{0,1:T(8,128)(2,1)} %bitcast.8) | data formatting | bytes 1179648
  108.7 0.0 copy-done.1
  108.7 0.0 copy-start.2
  108.7 0.8 copy.21
  109.5 0.0 copy-done
  109.5 0.8 copy.22
  110.3 0.0 copy-done.2
  110.3 0.6 copy.23
Async XLA Ops:
  106.6 2.0 %copy-start.1 = (bf16[576,512]{1,0:T(8,128)(2,1)S(1)}, bf16[576,512]{1,0:T(8,128)(2,1)}, u32[]{:S(2)}) copy-start(bf16[576,512]{1,0:T(8,128)(2,1)} %get-tuple-element.9) | copy-start | bytes 1769476
  106.6 2.8 %copy-start = (bf16[576,512]{1,0:T(8,128)(2,1)S(1)}, bf16[576,512]{1,0:T(8,128)(2,1)}, u32[]{:S(2)}) copy-start(bf16[576,512]{1,0:T(8,128)(2,1)} %get-tuple-element.10) | copy-start | bytes 1769476
  108.7 1.6 %copy-start.2 = (bf16[9,1152]{1,0:T(8,128)(2,1)S(1)}, bf16[9,1152]{1,0:T(8,128)(2,1)}, u32[]{:S(2)}) copy-start(bf16[9,1152]{1,0:T(8,128)(2,1)} %get-tuple-element.19) | copy-start | bytes 62212

commit v3 on v2

--- a/solution.py
+++ b/solution.py
@@ -29,8 +29,8 @@
 
 (
     W_Z, W_Y0, W_X0, W_C0, W_Y1, W_X1, W_C1, SEND_A, SEND_B, SEND_C, BACK_A, BACK_B,
-    G_C0, G_X0, G_Y0, G_C1, G_X1, G_Y1, G_Z, G_H, G_F, OWN, LOAD,
-) = range(23)
+    G_C0, G_X0, G_Y0, G_C1, G_X1, G_Y1, G_Z0, G_Z1, G_H, G_F, OWN, LOAD,
+) = range(24)
 STAGES = 40
 
 ATT, DV, DQ, DK = (0, 72), (144, 360), (216, 432), (288, 504)
@@ -72,6 +72,14 @@
     return m
 
 
+def spread_zz():
+    m = np.zeros((32, 32), np.float32)
+    for zz in range(2):
+        for i in range(SHARE):
+            m[zz * 16 + i, zz * 9 + i] = 1
+    return m
+
+
 def dot(a, b, ca, cb):
     return lax.dot_general(a, b, (((ca,), (cb,)), ((), ())), preferred_element_type=F32)
 
@@ -93,11 +101,11 @@
 
 def kernel(
     q_hbm, k_hbm, v_hbm, w_ref, cot_hbm,
-    rows_m, side_m, side_t, gx_m, gx_t, gy_m, gy_t,
+    rows_m, side_m, side_t, gx_m, gx_t, gz_m, gy_t,
     dq_hbm, dk_hbm, dv_hbm, wg_ref,
     q_ref, k_ref, v_ref, cot_ref, dq_ref, dk_ref, dv_ref,
     wpad, g1, c1, g2, c2, wall, up, msg_t, msg, got, grp, prob, sprob, res, out_msg, back,
-    att, part, rc, xs, rx, ys, ry, zs, zp, rz, rh, fw,
+    att, part, rc, xs, rx, ys, ry, zp, rz, rh, fw,
     send, recv,
 ):
     me, d = lax.axis_index("frame"), lax.axis_index("dp")
@@ -279,9 +287,24 @@
             put(ys.at[h, rows16(lax.rem(y + i, 4), 32)], ry.at[h, y], stage + 2, on_y(i))
         ry[h, y] = ys[h, rows16(y, 32), :]
 
-    def grad_sum(h, stage):
+    def grad_z(h, stage):
         arrived(ry.at[h, 0:3], stage + 2)
-        zs[32 * h : 32 * (h + 1), :] = total(ry, h).astype(BF)
+        zp[h] = move(gz_m[...], total(ry, h).astype(BF))
+        for zz in range(2):
+
+            @pl.when(z != 2 * h + zz)
+            def _(zz=zz):
+                to = frame((2 * h + zz) * 16 + y * 4 + x)
+                put(zp.at[h, 16 * zz : 16 * (zz + 1)], rz.at[0, z], G_Z0 + h, to)
+
+    def grad_h(h):
+        @pl.when(lax.div(z, 2) == h)
+        def _():
+            rz[0, z] = zp[h, rows16(z - 2 * h), :]
+            arrived(rz.at[0, 0:3], G_Z0 + h)
+            rh[0, zhi] = total(rz, 0).astype(BF)
+            for i in range(1, 4):
+                put(rh.at[0, zhi], rh.at[0, zhi], G_H, on_zhi(i))
 
     lax.fori_loop(0, 2, clip_forward, 0)
     w_core(1)
@@ -395,25 +418,18 @@
         G_C1,
     )
     send_back(BACK, MSG, BACK_B, 11, 21)
-    grad_sum(0, G_C0)
+    grad_z(0, G_C0)
     grad_x(1, G_C1)
     send_back(BACK, MSG, BACK_B, 21, F // 2)
     clip_backward(1, 0)
     grad_y(1, G_C1)
+    grad_h(0)
     stores = []
     for n, (src, dst) in enumerate(((dq_ref, dq_hbm), (dk_ref, dk_hbm), (dv_ref, dv_hbm))):
         stores.append(pltpu.make_async_copy(src.at[tops], dst.at[tops], recv.at[LOAD + 7 + n]))
         stores[-1].start()
-    grad_sum(1, G_C1)
-
-    zp[...] = move(gy_m[...], zs[...])
-    for i in range(1, 4):
-        put(zp.at[rows16(lax.rem(z + i, 4))], rz.at[0, z], G_Z, on_z(i))
-    rz[0, z] = zp[rows16(z), :]
-    arrived(rz.at[0, 0:3], G_Z)
-    rh[0, zhi] = total(rz, 0).astype(BF)
-    for i in range(1, 4):
-        put(rh.at[0, zhi], rh.at[0, zhi], G_H, on_zhi(i))
+    grad_z(1, G_C1)
+    grad_h(1)
 
     arrived(got.at[0 : 16 * (F - 1), BACK:MSG], BACK_B)
     for hp in range(2):
@@ -446,7 +462,9 @@
         sent(rc.at[h], stage)
         sent(rx.at[h, 0:3], stage + 1)
         sent(ry.at[h, 0:3], stage + 2)
-    sent(rz.at[0, 0:3], G_Z)
+    for h in range(2):
+        pl.when(lax.div(z, 2) == h)(lambda h=h: sent(rz.at[0, 0:1], G_Z0 + h))
+        pl.when(lax.div(z, 2) != h)(lambda h=h: sent(rz.at[0, 0:2], G_Z0 + h))
     sent(rh.at[0, 0:3], G_H)
     sent(fw.at[:, 0:OFF], G_F)
     for copy in stores:
@@ -457,7 +475,7 @@
     tables = [
         jnp.asarray(m, BF)
         for m in (
-            group_rows(), side_rows(), side_rows().T, spread_y(), spread_y().T, spread_z(), spread_z().T,
+            group_rows(), side_rows(), side_rows().T, spread_y(), spread_y().T, spread_zz(), spread_z().T,
         )
     ]
     vmem, hbm = pl.BlockSpec(memory_space=pltpu.VMEM), pl.BlockSpec(memory_space=pl.ANY)
@@ -490,8 +508,7 @@
             ((2, 4, 80, WIN), BF),
             ((2, 128, WIN), BF),
             ((2, 4, 32, WIN), BF),
-            ((64, WIN), BF),
-            ((64, WIN), BF),
+            ((2, 32, WIN), BF),
             ((1, 4, 16, WIN), BF),
             ((1, 4, 16, WIN), BF),
             ((16, D), F32),

time: 111 us -> 107 us (0.964)
  the two profiles are of different devices: /device:TPU:1 before, /device:TPU:65 now
where the time goes in v3:
time: 107 us
  Pallas kernels  102 us (95%)
  local copies, waits for them, and re-layouts  4.27 us (4%)
    pallas_call x1, Pallas kernels, on_device(): pl.pallas_call(kernel, out_shape=(turned, turned, turned, jax.ShapeDtypeS...  102 us
    unnamed x10, local copies, waits for them, and re-layouts  4.27 us

profile of v3, /device:TPU:65, one launch (start us, length us, event | category | flops | bytes accessed | tf_op | source)
XLA Modules:
  0.0 107.0 jit_solution(7526760294379988580)
XLA Ops:
  0.6 102.1 %shard_map.147 = (bf16[576,512]{1,0:T(8,128)(2,1)}, bf16[576,512]{1,0:T(8,128)(2,1)}, bf16[576,512]{1,0:T(8,128)(2,1)}, bf16[9,1152]{1,0:T(8,128)(2,1)}) custom-call(bf16[576,512]{1,0:T(8,128)(2,1)} %bitcast.9, bf16[576,512]{1,0:T(8,128)(2,1)} %bitcast.10, bf16[576,512]{1,0:T(8,128)(2,1)} %bitcast.11, bf16[9,1152]{1,0:T(8,128)(2,1)} %w_ref.1, ...), custom_call_target="tpu_custom_call" | custom-call | flops 4000000000 | bytes 6000000 | tf_op jit(solution)/shard_map/pallas_call | solution.py:517
  102.7 0.0 copy-start.1
  102.7 0.0 copy-start
  102.7 2.0 %copy.20 = bf16[512,576]{0,1:T(8,128)(2,1)} copy(bf16[512,576]{0,1:T(8,128)(2,1)} %bitcast.8) | data formatting | bytes 1179648
  104.8 0.0 copy-done.1
  104.8 0.0 copy-start.2
  104.8 0.8 copy.21
  105.6 0.0 copy-done
  105.6 0.8 copy.22
  106.4 0.0 copy-done.2
  106.4 0.6 copy.23
Async XLA Ops:
  102.7 2.0 %copy-start.1 = (bf16[576,512]{1,0:T(8,128)(2,1)S(1)}, bf16[576,512]{1,0:T(8,128)(2,1)}, u32[]{:S(2)}) copy-start(bf16[576,512]{1,0:T(8,128)(2,1)} %get-tuple-element.9) | copy-start | bytes 1769476
  102.7 2.8 %copy-start = (bf16[576,512]{1,0:T(8,128)(2,1)S(1)}, bf16[576,512]{1,0:T(8,128)(2,1)}, u32[]{:S(2)}) copy-start(bf16[576,512]{1,0:T(8,128)(2,1)} %get-tuple-element.10) | copy-start | bytes 1769476
  104.8 1.6 %copy-start.2 = (bf16[9,1152]{1,0:T(8,128)(2,1)S(1)}, bf16[9,1152]{1,0:T(8,128)(2,1)}, u32[]{:S(2)}) copy-start(bf16[9,1152]{1,0:T(8,128)(2,1)} %get-tuple-element.19) | copy-start | bytes 62212

commit v4 on v3

--- a/solution.py
+++ b/solution.py
@@ -410,17 +410,16 @@
     clip_backward(0, 0)
 
     sent(got.at[0 : 16 * (F - 1), 0:BACK], BACK_A)
-    send_back(BACK, MSG, BACK_B, 0, 11)
     arrived(got.at[0 : 16 * (F - 1), 0:BACK], BACK_A)
     grad_core(
         1,
         dot(side_m[:, 0:PAIR], back[0, :, 0:PAIR], 1, 1) + dot(side_m[:, PAIR:SIDE], back[1, :, 0:PAIR], 1, 1),
         G_C1,
     )
-    send_back(BACK, MSG, BACK_B, 11, 21)
+    send_back(BACK, MSG, BACK_B, 0, 18)
     grad_z(0, G_C0)
     grad_x(1, G_C1)
-    send_back(BACK, MSG, BACK_B, 21, F // 2)
+    send_back(BACK, MSG, BACK_B, 18, F // 2)
     clip_backward(1, 0)
     grad_y(1, G_C1)
     grad_h(0)
@@ -469,6 +468,11 @@
     sent(fw.at[:, 0:OFF], G_F)
     for copy in stores:
         copy.wait()
+
+
+def copy_out(a, b, c, d, to_a, to_b, to_c, to_d):
+    for src, dst in ((a, to_a), (b, to_b), (c, to_c), (d, to_d)):
+        dst[...] = src[...]
 
 
 def on_device(queries, key_vectors, values, w_out, cotangent):
@@ -526,6 +530,12 @@
         ),
         cost_estimate=pl.CostEstimate(flops=4_000_000_000, bytes_accessed=6_000_000, transcendentals=2_000_000),
     )(queries.T, key_vectors.T, values.T, w_out, cotangent, *tables)
+    dq, dk, dv, wg = pl.pallas_call(
+        copy_out,
+        out_shape=(turned, turned, turned, jax.ShapeDtypeStruct((SHARE, D), BF)),
+        in_specs=[vmem] * 4,
+        out_specs=(vmem,) * 4,
+    )(dq, dk, dv, wg)
     return dq.T, dk.T, dv.T, wg
 
 

time: 107 us -> 106 us (level)
  local copies, waits for them, and re-layouts: 4.27 us -> 0 us
  Pallas kernels: 102 us -> 105 us
    unnamed x10 -> x0, local copies, waits for them, and re-layouts: 4.27 us -> none
    pallas_call x0 -> x1, Pallas kernels: none -> 2.67 us  [on_device(): pl.pallas_call(copy_out, out_shape=(turned, turned, turned, jax.ShapeDtyp...]
where the time goes in v4:
time: 106 us; the launch traced here: 105 us
  Pallas kernels  105 us (99%)
    pallas_call x1, Pallas kernels, on_device(): pl.pallas_call(kernel, out_shape=(turned, turned, turned, jax.ShapeDtypeS...  102 us
    pallas_call x1, Pallas kernels, on_device(): pl.pallas_call(copy_out, out_shape=(turned, turned, turned, jax.ShapeDtyp...  2.67 us

profile of v4, /device:TPU:65, one launch (start us, length us, event | category | flops | bytes accessed | tf_op | source)
XLA Modules:
  0.0 105.4 jit_solution(3823958745789790420)
XLA Ops:
  0.6 102.1 %shard_map.147 = (bf16[576,512]{1,0:T(8,128)(2,1)}, bf16[576,512]{1,0:T(8,128)(2,1)}, bf16[576,512]{1,0:T(8,128)(2,1)}, bf16[9,1152]{1,0:T(8,128)(2,1)}) custom-call(bf16[576,512]{1,0:T(8,128)(2,1)} %bitcast.6, bf16[576,512]{1,0:T(8,128)(2,1)} %bitcast.7, bf16[576,512]{1,0:T(8,128)(2,1)} %bitcast.8, bf16[9,1152]{1,0:T(8,128)(2,1)} %w_ref.1, ...), custom_call_target="tpu_custom_call" | custom-call | flops 4000000000 | bytes 6000000 | tf_op jit(solution)/shard_map/pallas_call | solution.py:521
  102.8 2.7 %shard_map.148 = (bf16[576,512]{1,0:T(8,128)(2,1)}, bf16[576,512]{1,0:T(8,128)(2,1)}, bf16[576,512]{1,0:T(8,128)(2,1)}, bf16[9,1152]{1,0:T(8,128)(2,1)}) custom-call(bf16[576,512]{1,0:T(8,128)(2,1)} %get-tuple-element.12.a, bf16[576,512]{1,0:T(8,128)(2,1)} %get-tuple-element.13.b, bf16[576,512]{1,0:T(8,128)(2,1)} %get-tuple-element.14.c, ...), custom_call_target="tpu_custom_call" | custom-call | tf_op jit(solution)/shard_map/pallas_call | solution.py:533
